TPU v7x, 128 devices: a whole 4x4x4 slice. The times are simulated.
128 devices in a mesh: machine: 8 (over x, core), dev: 16 (over y, z).
Axes of the slice: x: 4, y: 4, z: 4, core: 2. Of those that a mesh axis runs over, the one named last changes fastest.
Arguments:
- embed: bfloat16 [786432, 128], P(('machine', 'dev'))
- cotangent: float32 [786432, 128], P(('machine', 'dev'))
- degrees: int32 [786432], P(('machine', 'dev')), may hold values from 16 to 256
- send_rows: int32 [128, 128, 32], P(('machine', 'dev')), may hold values from -1 to 6143, as said below
- inner_tiles: bfloat16 [6144, 4, 128, 128], P(('machine', 'dev')), may hold values from 0 to 1, as said below
- inner_src: int32 [6144, 4], P(('machine', 'dev')), may hold values from 0 to 47
- border_tiles: bfloat16 [6144, 4, 128, 128], P(('machine', 'dev')), may hold values from 0 to 1, as said below
- border_src: int32 [6144, 4], P(('machine', 'dev')), may hold values from 0 to 31
Outputs:
- final: bfloat16 [786432, 128], P(('machine', 'dev'))
- grad: float32 [786432, 128], P(('machine', 'dev'))
Inputs may be any that keep to these rules, and one draw needn't show every extreme that they name: `send_rows`: -1 marks an empty slot; live slots of a pair come first. No partition sends to itself; every partition p fills all 32 slots for partition (p + 1) mod 128, and each other pair holds 1 to 32 live slots. `inner_tiles`: entries are 0 or 1. `border_tiles`: entries are 0 or 1.
All inputs are finite; a program needn't handle non-finite values.
Results may differ from a plain program's by a relative error of at most 0.002.
Values may be sent and summed in bfloat16 or wider, within the bound.
A program may use at most 128 MiB of HBM per device.

v0:
```python
import functools

import jax
import jax.numpy as jnp
from jax import lax
from jax.experimental import pallas as pl
from jax.experimental.pallas import tpu as pltpu
from jax.sharding import PartitionSpec as P

F32 = jnp.float32
BF16 = jnp.bfloat16
I32 = jnp.int32
THIRD = 1.0 / 3.0
TRANS = (((0,), (0,)), ((), ()))
LANES = (((1,), (1,)), ((), ()))
MESH = pl.DeviceIdType.MESH
ANY = pl.BlockSpec(memory_space=pl.ANY)
VM = pl.BlockSpec(memory_space=pltpu.VMEM)
SM = pl.BlockSpec(memory_space=pltpu.SMEM)
GROUPS = 64
DEAD = GROUPS - 1


def rows_at(index, size):
    return pl.ds(pl.multiple_of(index * size, size), size)


def iota(shape, axis):
    return lax.broadcasted_iota(I32, shape, axis)


def as_bf16(mask):
    return mask.astype(F32).astype(BF16)


def kept(flag, value):
    flags = jnp.broadcast_to(flag, value.shape)
    return jnp.where(flags > 0, value, 0.0)


def joined(flag, before, value):
    flags = jnp.broadcast_to(flag, value.shape)
    return jnp.where(flags > 0, before + value, value)


def group_ranks(groups, hot_ref, counted_ref):
    chunks = len(groups)
    row = iota((GROUPS, 128), 0)
    for c in range(chunks):
        hot_ref[c * GROUPS : (c + 1) * GROUPS, :] = as_bf16(groups[c] == row)
    before = as_bf16(iota((128, 128), 0) < iota((128, 128), 1))
    weights = jnp.concatenate([before, jnp.ones((128, 128), BF16)], axis=1)
    size = chunks * GROUPS
    counted_ref[:size, :] = jnp.dot(hot_ref[:size, :], weights, preferred_element_type=F32)
    total = jnp.zeros((GROUPS, 128), F32)
    for c in range(chunks):
        total = total + counted_ref[c * GROUPS : (c + 1) * GROUPS, 128:]
    lower = (iota((GROUPS, GROUPS), 1) < iota((GROUPS, GROUPS), 0)).astype(F32)
    start = jnp.dot(lower, total, precision=lax.Precision.HIGHEST, preferred_element_type=F32)
    running = start
    ranks = []
    later = []
    for c in range(chunks):
        part = slice(c * GROUPS, (c + 1) * GROUPS)
        hot = hot_ref[part, :].astype(F32)
        rank = jnp.sum(hot * (counted_ref[part, :128] + running), axis=0, keepdims=True)
        ranks.append(rank.astype(I32))
        later.append((rank > jnp.sum(hot * start, axis=0, keepdims=True)).astype(I32))
        running = running + counted_ref[part, 128:]
    return ranks, later, (start + total).astype(I32)


def place(ranks, rows, values):
    row = iota((rows, 128), 0)
    square = iota((128, 128), 0)
    placed = jnp.zeros((rows * len(values[0]), 128), F32)
    for rank, chunk_values in zip(ranks, values):
        high = (jnp.right_shift(rank, 7) == row).astype(F32)
        left = jnp.concatenate([high * value.astype(F32) for value in chunk_values], axis=0)
        right = as_bf16((rank & 127) == square)
        placed = placed + lax.dot_general(
            left.astype(BF16), right, LANES, preferred_element_type=F32
        )
    placed = placed.astype(I32)
    return [placed[i * rows : (i + 1) * rows] for i in range(len(values[0]))]


def split_table(table, chunks):
    parts = []
    first = 0
    for size in (chunks, chunks, 8, GROUPS, 24, GROUPS, 24, GROUPS):
        parts.append(table.at[pl.ds(first, size)])
        first += size
    return parts


def order_kernel(
    nodes, pers, slots_ref, sources_ref,
    table_out, nodes_out, hot_ref, counted_ref,
):
    chunks = slots_ref.shape[0]
    pick_out, order_out, path_out, stop_out, in_out, in_ends, bd_out, bd_ends = split_table(
        table_out, chunks
    )
    lane = iota((1, 128), 1)
    index = slots_ref[...]
    pick_out[...] = jnp.where(index < 0, nodes, index)
    low = index & 127
    high = jnp.where(index < 0, DEAD, jnp.right_shift(index, 7))
    groups = [high[c : c + 1] for c in range(chunks)]
    ranks, _, ends = group_ranks(groups, hot_ref, counted_ref)
    row = iota((GROUPS, 128), 0)
    step = iota((GROUPS, 128), 1)
    stop = row + jnp.maximum(jnp.right_shift(ends + 127, 7) - 1, 0)
    stop_out[...] = stop + 1
    live = row < nodes // 128
    passed = (live & (stop < step)).astype(F32)
    block = jnp.sum(passed, axis=0, keepdims=True).astype(I32)
    passed_before = (live & (stop < step - 1)).astype(F32)
    block_before = jnp.sum(passed_before, axis=0, keepdims=True).astype(I32)
    chunk = jnp.minimum(lane - block, chunks - 1)
    path_out[...] = jnp.concatenate(
        [chunk, block * 128, (block == block_before).astype(I32)] + [block] * 5, axis=0
    )
    values = [
        [jnp.full((1, 128), c, I32), lane, low[c : c + 1], groups[c]] for c in range(chunks)
    ]
    slot_chunk, slot_lane, node_low, node_high = place(ranks, chunks, values)
    order_out[...] = slot_chunk * 128 + slot_lane
    nodes_out[...] = node_high * 128 + node_low
    for part, out, out_ends in ((0, in_out, in_ends), (1, bd_out, bd_ends)):
        groups = [sources_ref[part * 2 + c : part * 2 + c + 1, :] for c in range(2)]
        ranks, later, ends = group_ranks(groups, hot_ref, counted_ref)
        before = jnp.concatenate([jnp.zeros((1, 128), I32), ends[:-1]], axis=0)
        out_ends[...] = jnp.where(iota((GROUPS, 128), 1) == 1, ends - before, ends)
        shift = pers[part].bit_length() - 1
        values = [
            [lane + c * 128, later[c], jnp.right_shift(lane + c * 128, shift)] for c in range(2)
        ]
        for i, placed in enumerate(place(ranks, 8, values)):
            out[i * 8 : i * 8 + 8, :] = placed


def hop_kernel(
    machines, devs, blocks, border_blocks, per_in, per_bd, slots,
    index_table, inner_src, border_src, nodes_ref, degrees, embed_hbm, cotangent_hbm, inner_hbm, border_hbm,
    final_ref, grad_ref,
    inner, border, run, table, root_ref, root_row, u, x, embed, total, mean, wide, sorted_rows,
    out_g0, out_g1, out_x0, out_x1, in_g0, in_g1, in_x0, in_x1, copy_sem, send_sem, recv_sem,
):
    nodes = blocks * 128
    peers = 128 // slots
    out_g, out_x, in_g, in_x = (out_g0, out_g1), (out_x0, out_x1), (in_g0, in_g1), (in_x0, in_x1)
    chunks = border_blocks
    pick, order, path, stop, in_order, in_ends, bd_order, bd_ends = split_table(index_table, chunks)
    count = machines * devs
    my_m = lax.axis_index("machine")
    my_d = lax.axis_index("dev")
    me = my_m * devs + my_d
    rows_of_devs = devs // peers

    copies = [
        pltpu.make_async_copy(src, dst, copy_sem.at[i])
        for i, (src, dst) in enumerate(
            (
                (cotangent_hbm, grad_ref),
                (border_hbm, border),
                (embed_hbm, embed),
                (inner_hbm, inner),
            )
        )
    ]
    for copy in copies:
        copy.start()

    barrier = pltpu.get_barrier_semaphore()

    def greet(step, carry):
        pm = (my_m + step // devs) % machines
        pd = (my_d + step % devs) % devs
        pl.semaphore_signal(barrier, inc=1, device_id=(pm, pd), device_id_type=MESH)
        return carry

    lax.fori_loop(1, count, greet, 0)
    for buffer in in_g:
        buffer[pl.ds(me, 1)] = jnp.zeros((1, slots, 128), BF16)
    for buffer in in_x:
        buffer[pl.ds(my_m * rows_of_devs + my_d // peers, 1), pl.ds(my_d % peers, 1)] = jnp.zeros((1, 1, slots, 128), BF16)

    def send_all(kind, hop, out_buffer, in_buffer, fill):
        out_ref = out_buffer[hop]
        in_ref = in_buffer[hop]
        if kind == 0:
            mine = in_ref.at[me]
        else:
            mine = in_ref.at[my_m * rows_of_devs + my_d // peers, my_d % peers]

        def step(j, carry):
            offset = (j * 13) % chunks
            pm = (my_m + offset // rows_of_devs) % machines
            pr = (my_d // peers + offset % rows_of_devs) % rows_of_devs
            chunk = pm * rows_of_devs + pr
            out_ref[pl.ds(chunk * peers, peers)] = fill(chunk).reshape(peers, slots, 128)
            for q in range(peers):
                pd = pr * peers + (my_d + q) % peers
                peer = pm * devs + pd

                @pl.when(peer != me)
                def _():
                    pltpu.make_async_remote_copy(
                        src_ref=out_ref.at[peer],
                        dst_ref=mine,
                        send_sem=send_sem.at[kind, hop],
                        recv_sem=recv_sem.at[kind, hop],
                        device_id=(pm, pd),
                        device_id_type=MESH,
                    ).start()

            return carry

        lax.fori_loop(0, chunks, step, 0)

    def wait_for(buffer, hop, sem):
        most = buffer[hop].at[pl.ds(0, count - 1)]
        pltpu.make_async_copy(most, most, sem).wait()

    def grouped_tiles(tiles, tile_order, per, field):
        def body(t, carry):
            row, lane = t // 128, t % 128
            tile = tile_order[row, lane]
            after = tile_order[8 + row, lane]
            block = field[tile_order[16 + row, lane]]
            product = lax.dot_general(tiles[tile], block, TRANS, preferred_element_type=F32)
            run[t + 1] = joined(after, run[t], product)
            return carry

        run[0] = jnp.zeros((128, 128), F32)
        lax.fori_loop(0, blocks * per, body, 0, unroll=16)

    def grouped_sum(tile_ends, c):
        return kept(tile_ends[c, 1], run[tile_ends[c, 0]])

    def send_sums(hop):
        grouped_tiles(border, bd_order, per_bd, u)
        if hop == 0:
            pl.semaphore_wait(barrier, count - 1)
        send_all(0, hop, out_g, in_g, lambda c: grouped_sum(bd_ends, c).astype(BF16))

    sub = iota((8, 128), 0)

    def gather_chunk(which, source, chunk):
        parts = []
        for g in range(16):
            part = None
            for r in range(8):
                row = source[pl.ds(which[chunk, g * 8 + r], 1), :]
                row = jnp.broadcast_to(row, (8, 128))
                part = row if part is None else jnp.where(sub == r, row, part)
            parts.append(part)
        return jnp.concatenate(parts, axis=0).astype(BF16)

    def send_rows(hop):
        send_all(1, hop, out_x, in_x, lambda c: gather_chunk(pick, table, c))

    def inner_back():
        grouped_tiles(inner, in_order, per_in, u)

        def body(c, carry):
            total[rows_at(c, 128), :] = grouped_sum(in_ends, c)
            return carry

        lax.fori_loop(0, blocks, body, 0, unroll=4)

    def inner_forward():
        def body(b, carry):
            lhs = jnp.concatenate([inner[b * per_in + k] for k in range(per_in)], axis=1)
            rhs = [x[inner_src[b * per_in + k]] for k in range(per_in)]
            table[rows_at(b, 128), :] = jnp.dot(
                lhs, jnp.concatenate(rhs, axis=0), preferred_element_type=F32
            )
            return carry

        lax.fori_loop(0, blocks, body, 0, unroll=16)

    def border_forward(hop, finish):
        wait_for(out_x, hop, recv_sem.at[1, hop])

        def body(b, carry):
            lhs = jnp.concatenate([border[b * per_bd + k] for k in range(per_bd)], axis=1)
            rhs = [
                in_x[hop][border_src[b * per_bd + k]].reshape(128, 128)
                for k in range(per_bd)
            ]
            value = jnp.dot(lhs, jnp.concatenate(rhs, axis=0), preferred_element_type=F32)
            where = rows_at(b, 128)
            finish(b, root_ref[where, :] * (table[where, :] + value))
            return carry

        lax.fori_loop(0, blocks, body, 0, unroll=16)

    def gather_back(hop, finish):
        wait_for(in_g, hop, recv_sem.at[0, hop])

        def widen(c, carry):
            rows = in_g[hop][pl.ds(c * peers, peers)].reshape(128, 128)
            wide[rows_at(c, 128), :] = rows.astype(F32)
            return carry

        lax.fori_loop(0, chunks, widen, 0, unroll=2)

        def sort_rows(c, carry):
            sorted_rows[c] = gather_chunk(order, wide, c)
            return carry

        lax.fori_loop(0, chunks, sort_rows, 0)
        square = iota((128, 128), 0)

        run[0] = jnp.zeros((128, 128), F32)

        def merge(step, carry):
            c = path[0, step]
            hot = as_bf16(nodes_ref[pl.ds(c, 1), :] == square + path[1, step])
            part = jnp.dot(hot, sorted_rows[c], preferred_element_type=F32)
            run[step + 1] = joined(path[2, step], run[step], part)
            return carry

        lax.fori_loop(0, chunks + blocks, merge, 0, unroll=8)

        def body(d, carry):
            where = rows_at(d, 128)
            finish(d, root_ref[where, :] * (total[where, :] + run[stop[d, 0]]))
            return carry

        lax.fori_loop(0, blocks, body, 0, unroll=4)

    root_row[...] = lax.rsqrt(degrees[...].astype(F32))
    copies[0].wait()

    def first_u(b, carry):
        where = rows_at(b, 128)
        root = jnp.broadcast_to(root_row[pl.ds(b, 1), :], (128, 128)).T
        root_ref[where, :] = root
        u[b] = (root * grad_ref[where, :]).astype(BF16)
        return carry

    lax.fori_loop(0, blocks, first_u, 0, unroll=4)
    copies[1].wait()
    send_sums(0)
    copies[2].wait()

    def first_x(b, carry):
        where = rows_at(b, 128)
        value = (root_ref[where, :] * embed[where, :].astype(F32)).astype(BF16)
        x[b] = value
        table[where, :] = value.astype(F32)
        return carry

    lax.fori_loop(0, blocks, first_x, 0, unroll=4)
    table[pl.ds(nodes, 8), :] = jnp.zeros((8, 128), F32)
    send_rows(0)
    copies[3].wait()
    inner_back()
    inner_forward()

    def next_u(b, back):
        where = rows_at(b, 128)
        grad_ref[where, :] = grad_ref[where, :] + back
        u[b] = (root_ref[where, :] * back).astype(BF16)

    gather_back(0, next_u)
    send_sums(1)

    def next_x(b, hop_one):
        where = rows_at(b, 128)
        mean[where, :] = embed[where, :].astype(F32) + hop_one
        value = (root_ref[where, :] * hop_one).astype(BF16)
        x[b] = value
        table[where, :] = value.astype(F32)

    border_forward(0, next_x)
    send_rows(1)
    inner_back()
    inner_forward()

    def end_u(b, back):
        where = rows_at(b, 128)
        grad_ref[where, :] = (grad_ref[where, :] + back) * THIRD

    gather_back(1, end_u)

    def end_x(b, hop_two):
        where = rows_at(b, 128)
        final_ref[where, :] = ((mean[where, :] + hop_two) * THIRD).astype(BF16)

    border_forward(1, end_x)
    for hop in range(2):
        wait_for(out_g, hop, send_sem.at[0, hop])
        wait_for(out_x, hop, send_sem.at[1, hop])


def per_device(
    embed, cotangent, degrees, send_rows, inner_tiles, inner_src, border_tiles, border_src
):
    peers, slots = send_rows.shape[1:]
    nodes, width = embed.shape
    blocks, per_in = inner_src.shape
    per_bd = border_src.shape[1]
    machines = lax.axis_size("machine")
    devs = lax.axis_size("dev")
    chunks = peers * slots // 128
    in_src = inner_src.reshape(-1)
    bd_src = border_src.reshape(-1)
    sources = jnp.stack([jnp.pad(s, (0, 256 - s.size), constant_values=DEAD) for s in (in_src, bd_src)])
    index_rows = 2 * chunks + 3 * GROUPS + 56
    index_table, sorted_nodes = pl.pallas_call(
        functools.partial(order_kernel, nodes, (per_in, per_bd)),
        out_shape=(
            jax.ShapeDtypeStruct((index_rows, 128), I32),
            jax.ShapeDtypeStruct((chunks, 128), I32),
        ),
        in_specs=[VM, VM],
        out_specs=(VM, VM),
        scratch_shapes=[
            pltpu.VMEM((chunks * GROUPS, 128), BF16),
            pltpu.VMEM((chunks * GROUPS, 256), F32),
        ],
        compiler_params=pltpu.CompilerParams(vmem_limit_bytes=16 * 2**20),
        name="order",
    )(send_rows.reshape(chunks, 128), sources.reshape(4, 128))

    buffer = pltpu.VMEM((peers, slots, width), BF16)
    by_row = pltpu.VMEM((chunks, 128 // slots, slots, width), BF16)
    final, grad = pl.pallas_call(
        functools.partial(
            hop_kernel, machines, devs, blocks, chunks, per_in, per_bd, slots
        ),
        out_shape=(
            jax.ShapeDtypeStruct((nodes, width), BF16),
            jax.ShapeDtypeStruct((nodes, width), F32),
        ),
        in_specs=[SM] * 3 + [VM] * 2 + [ANY] * 4,
        out_specs=(VM, VM),
        scratch_shapes=[
            pltpu.VMEM((blocks * per_in, 128, 128), BF16),
            pltpu.VMEM((blocks * per_bd, 128, 128), BF16),
            pltpu.VMEM((blocks * max(per_in, per_bd) + 1, 128, 128), F32),
            pltpu.VMEM((nodes + 8, width), F32),
            pltpu.VMEM((nodes, width), F32),
            pltpu.VMEM((blocks, 128), F32),
            pltpu.VMEM((blocks, 128, width), BF16),
            pltpu.VMEM((blocks, 128, width), BF16),
            pltpu.VMEM((nodes, width), BF16),
            pltpu.VMEM((nodes, width), F32),
            pltpu.VMEM((nodes, width), F32),
            pltpu.VMEM((chunks * 128, width), F32),
            pltpu.VMEM((chunks, 128, width), BF16),
            *([buffer] * 6),
            by_row,
            by_row,
            pltpu.SemaphoreType.DMA((4,)),
            pltpu.SemaphoreType.DMA((2, 2)),
            pltpu.SemaphoreType.DMA((2, 2)),
        ],
        compiler_params=pltpu.CompilerParams(
            collective_id=0, has_side_effects=True, vmem_limit_bytes=62 * 2**20
        ),
        name="hops",
    )(
        index_table, in_src, bd_src, sorted_nodes, degrees.reshape(blocks, 128), embed, cotangent,
        inner_tiles.reshape(-1, 128, 128), border_tiles.reshape(-1, 128, 128),
    )
    return final, grad


def solution(mesh):
    both = ("machine", "dev")
    in_specs = (
        P(both, None),
        P(both, None),
        P(both),
        P(both, None, None),
        P(both, None, None, None),
        P(both, None),
        P(both, None, None, None),
        P(both, None),
    )
    out_specs = (P(both, None), P(both, None))
    return jax.shard_map(
        per_device, mesh=mesh, in_specs=in_specs, out_specs=out_specs, check_vma=False
    )
```

profile of v0, /device:TPU:1, one launch (start us, length us, event | category | flops | bytes accessed | tf_op | source)
XLA Modules:
  0.0 89.0 jit_solution(14823204979195022246)
XLA Ops:
  0.6 0.8 copy.12
  1.4 0.1 reshape.26.inner_src
  1.5 0.0 copy-start.3
  1.5 0.8 copy.13
  2.3 0.1 reshape.27.border_src
  2.4 0.0 copy-start.4
  2.4 0.8 copy.11
  3.3 0.1 reshape.25.slots_ref
  3.3 2.4 %order.1 = (s32[312,128]{1,0:T(8,128)S(1)}, s32[32,128]{1,0:T(8,128)S(1)}) custom-call(s32[32,128]{1,0:T(8,128)S(1)} %reshape.25.slots_ref, s32[4,128]{1,0:T(4,128)S(1)} %reshape.28.sources_ref), custom_call_target="tpu_custom_call" | custom-call | tf_op jit(solution)/shard_map/order/pallas_call | solution.py:415
  5.7 0.0 copy-start
  5.7 0.7 copy-done
  6.4 0.0 copy-start.1
  6.4 0.6 copy-done.1
  7.0 0.0 copy-done.3
  7.0 0.0 copy-done.4
  7.0 77.5 %hops.1 = (bf16[6144,128]{1,0:T(8,128)(2,1)}, f32[6144,128]{1,0:T(8,128)}) custom-call(s32[312,128]{1,0:T(8,128)} %copy-done, s32[192]{0:T(256)} %copy-done.3, s32[192]{0:T(256)} %copy-done.4, s32[32,128]{1,0:T(8,128)} %copy-done.1, s32[48,128]{1,0:T(8,128)} %bitcast.7, bf16[6144,128]{1,0:T(8,128)(2,1)} %embed_hbm.1, f32[6144,128]{1,0:T(8,128)} %cotangent_hbm.1, ...), custom_call_target="tpu_custom_call" | custom-call | tf_op jit(solution)/shard_map/hops/pallas_call | solution.py:433
  84.5 0.0 copy-start.2
  84.5 2.8 %copy.16 = bf16[6144,128]{1,0:T(8,128)(2,1)} copy(bf16[6144,128]{1,0:T(8,128)(2,1)} %get-tuple-element.8) | data formatting | bytes 3145728
  87.3 0.0 copy-done.2
  87.3 1.7 %copy.17 = f32[6144,128]{1,0:T(8,128)} copy(f32[6144,128]{1,0:T(8,128)S(1)} %copy-done.2) | data formatting | bytes 6291456
  (4 shorter events, 0.0 us)
Async XLA Ops:
  1.5 5.5 %copy-start.3 = (s32[192]{0:T(256)}, s32[192]{0:T(256)S(1)}, u32[]{:S(2)}) copy-start(s32[192]{0:T(256)S(1)} %reshape.26.inner_src) | copy-start | bytes 2308
  2.4 4.6 %copy-start.4 = (s32[192]{0:T(256)}, s32[192]{0:T(256)S(1)}, u32[]{:S(2)}) copy-start(s32[192]{0:T(256)S(1)} %reshape.27.border_src) | copy-start | bytes 2308
  5.7 0.7 copy-start
  6.4 0.6 copy-start.1
  84.5 2.8 %copy-start.2 = (f32[6144,128]{1,0:T(8,128)S(1)}, f32[6144,128]{1,0:T(8,128)}, u32[]{:S(2)}) copy-start(f32[6144,128]{1,0:T(8,128)} %get-tuple-element.9) | copy-start | bytes 9437188
where the time goes:
time: 89.3 us; the launch traced here: 89 us
  Pallas kernels  79.9 us (89%)
  local copies, waits for them, and re-layouts  8.4 us (9%)
    pallas_call x1, Pallas kernels, per_device(): pl.pallas_call(functools.partial(hop_kernel, machines, devs, blocks, chun...  77.5 us
    unnamed x15, local copies, waits for them, and re-layouts  8.1 us
    pallas_call x1, Pallas kernels, per_device(): pl.pallas_call(functools.partial(order_kernel, nodes, (per_in, per_bd)),...  2.37 us

commit v1 on v0

--- a/solution.py
+++ b/solution.py
@@ -88,7 +88,7 @@
 def split_table(table, chunks):
     parts = []
     first = 0
-    for size in (chunks, chunks, 8, GROUPS, 24, GROUPS, 24, GROUPS):
+    for size in (chunks, chunks, chunks, 8, GROUPS, 24, GROUPS, 24, GROUPS):
         parts.append(table.at[pl.ds(first, size)])
         first += size
     return parts
@@ -96,10 +96,10 @@
 
 def order_kernel(
     nodes, pers, slots_ref, sources_ref,
-    table_out, nodes_out, hot_ref, counted_ref,
+    table_out, hot_ref, counted_ref,
 ):
     chunks = slots_ref.shape[0]
-    pick_out, order_out, path_out, stop_out, in_out, in_ends, bd_out, bd_ends = split_table(
+    nodes_out, pick_out, order_out, path_out, stop_out, in_out, in_ends, bd_out, bd_ends = split_table(
         table_out, chunks
     )
     lane = iota((1, 128), 1)
@@ -152,7 +152,7 @@
     peers = 128 // slots
     out_g, out_x, in_g, in_x = (out_g0, out_g1), (out_x0, out_x1), (in_g0, in_g1), (in_x0, in_x1)
     chunks = border_blocks
-    pick, order, path, stop, in_order, in_ends, bd_order, bd_ends = split_table(index_table, chunks)
+    _, pick, order, path, stop, in_order, in_ends, bd_order, bd_ends = split_table(index_table, chunks)
     count = machines * devs
     my_m = lax.axis_index("machine")
     my_d = lax.axis_index("dev")
@@ -235,7 +235,7 @@
             return carry
 
         run[0] = jnp.zeros((128, 128), F32)
-        lax.fori_loop(0, blocks * per, body, 0, unroll=16)
+        lax.fori_loop(0, blocks * per, body, 0, unroll=32)
 
     def grouped_sum(tile_ends, c):
         return kept(tile_ends[c, 1], run[tile_ends[c, 0]])
@@ -269,7 +269,7 @@
             total[rows_at(c, 128), :] = grouped_sum(in_ends, c)
             return carry
 
-        lax.fori_loop(0, blocks, body, 0, unroll=4)
+        lax.fori_loop(0, blocks, body, 0, unroll=8)
 
     def inner_forward():
         def body(b, carry):
@@ -306,7 +306,7 @@
             wide[rows_at(c, 128), :] = rows.astype(F32)
             return carry
 
-        lax.fori_loop(0, chunks, widen, 0, unroll=2)
+        lax.fori_loop(0, chunks, widen, 0, unroll=4)
 
         def sort_rows(c, carry):
             sorted_rows[c] = gather_chunk(order, wide, c)
@@ -324,14 +324,14 @@
             run[step + 1] = joined(path[2, step], run[step], part)
             return carry
 
-        lax.fori_loop(0, chunks + blocks, merge, 0, unroll=8)
+        lax.fori_loop(0, chunks + blocks, merge, 0, unroll=16)
 
         def body(d, carry):
             where = rows_at(d, 128)
             finish(d, root_ref[where, :] * (total[where, :] + run[stop[d, 0]]))
             return carry
 
-        lax.fori_loop(0, blocks, body, 0, unroll=4)
+        lax.fori_loop(0, blocks, body, 0, unroll=8)
 
     root_row[...] = lax.rsqrt(degrees[...].astype(F32))
     copies[0].wait()
@@ -343,7 +343,7 @@
         u[b] = (root * grad_ref[where, :]).astype(BF16)
         return carry
 
-    lax.fori_loop(0, blocks, first_u, 0, unroll=4)
+    lax.fori_loop(0, blocks, first_u, 0, unroll=8)
     copies[1].wait()
     send_sums(0)
     copies[2].wait()
@@ -355,7 +355,7 @@
         table[where, :] = value.astype(F32)
         return carry
 
-    lax.fori_loop(0, blocks, first_x, 0, unroll=4)
+    lax.fori_loop(0, blocks, first_x, 0, unroll=8)
     table[pl.ds(nodes, 8), :] = jnp.zeros((8, 128), F32)
     send_rows(0)
     copies[3].wait()
@@ -411,15 +411,12 @@
     in_src = inner_src.reshape(-1)
     bd_src = border_src.reshape(-1)
     sources = jnp.stack([jnp.pad(s, (0, 256 - s.size), constant_values=DEAD) for s in (in_src, bd_src)])
-    index_rows = 2 * chunks + 3 * GROUPS + 56
-    index_table, sorted_nodes = pl.pallas_call(
+    index_rows = 3 * chunks + 3 * GROUPS + 56
+    index_table = pl.pallas_call(
         functools.partial(order_kernel, nodes, (per_in, per_bd)),
-        out_shape=(
-            jax.ShapeDtypeStruct((index_rows, 128), I32),
-            jax.ShapeDtypeStruct((chunks, 128), I32),
-        ),
+        out_shape=jax.ShapeDtypeStruct((index_rows, 128), I32),
         in_specs=[VM, VM],
-        out_specs=(VM, VM),
+        out_specs=VM,
         scratch_shapes=[
             pltpu.VMEM((chunks * GROUPS, 128), BF16),
             pltpu.VMEM((chunks * GROUPS, 256), F32),
@@ -435,8 +432,8 @@
             hop_kernel, machines, devs, blocks, chunks, per_in, per_bd, slots
         ),
         out_shape=(
-            jax.ShapeDtypeStruct((nodes, width), BF16),
-            jax.ShapeDtypeStruct((nodes, width), F32),
+            pltpu.VMEM((nodes, width), BF16),
+            pltpu.VMEM((nodes, width), F32),
         ),
         in_specs=[SM] * 3 + [VM] * 2 + [ANY] * 4,
         out_specs=(VM, VM),
@@ -462,11 +459,11 @@
             pltpu.SemaphoreType.DMA((2, 2)),
         ],
         compiler_params=pltpu.CompilerParams(
-            collective_id=0, has_side_effects=True, vmem_limit_bytes=62 * 2**20
+            collective_id=0, has_side_effects=True, vmem_limit_bytes=56 * 2**20
         ),
         name="hops",
     )(
-        index_table, in_src, bd_src, sorted_nodes, degrees.reshape(blocks, 128), embed, cotangent,
+        index_table, in_src, bd_src, index_table, degrees.reshape(blocks, 128), embed, cotangent,
         inner_tiles.reshape(-1, 128, 128), border_tiles.reshape(-1, 128, 128),
     )
     return final, grad

time: 89.3 us -> 82.6 us (0.925)
  Pallas kernels: 79.9 us -> 75.1 us
  local copies, waits for them, and re-layouts: 8.4 us -> 6.14 us
    pallas_call x1, Pallas kernels: 77.5 us -> 72.7 us  [per_device(): pl.pallas_call(functools.partial(hop_kernel, machines, devs, blocks, chun...]
    unnamed x15 -> x11, local copies, waits for them, and re-layouts: 8.1 us -> 5.84 us
where the time goes in v1:
time: 82.6 us; the launch traced here: 81.9 us
  Pallas kernels  75.1 us (91%)
  local copies, waits for them, and re-layouts  6.14 us (7%)
    pallas_call x1, Pallas kernels, per_device(): pl.pallas_call(functools.partial(hop_kernel, machines, devs, blocks, chun...  72.7 us
    unnamed x11, local copies, waits for them, and re-layouts  5.84 us
    pallas_call x1, Pallas kernels, per_device(): pl.pallas_call(functools.partial(order_kernel, nodes, (per_in, per_bd)),...  2.37 us

profile of v1, /device:TPU:1, one launch (start us, length us, event | category | flops | bytes accessed | tf_op | source)
XLA Modules:
  0.0 81.9 jit_solution(15443624386317448622)
XLA Ops:
  0.6 0.8 copy.12
  1.4 0.1 reshape.26.inner_src
  1.5 0.0 copy-start.1
  1.5 0.8 copy.13
  2.3 0.1 reshape.27.border_src
  2.4 0.0 copy-start.2
  2.4 0.8 copy.11
  3.3 0.1 reshape.25.slots_ref
  3.3 2.4 %order.1.index_table.nodes_ref = s32[344,128]{1,0:T(8,128)S(1)} custom-call(s32[32,128]{1,0:T(8,128)S(1)} %reshape.25.slots_ref, s32[4,128]{1,0:T(4,128)S(1)} %reshape.28.sources_ref), custom_call_target="tpu_custom_call" | custom-call | tf_op jit(solution)/shard_map/order/pallas_call | solution.py:415
  5.7 0.0 copy-done.1
  5.7 0.0 copy-done.2
  5.7 0.0 copy-start
  5.7 0.7 copy-done
  6.4 72.7 %hops.1 = (bf16[6144,128]{1,0:T(8,128)(2,1)S(1)}, f32[6144,128]{1,0:T(8,128)S(1)}) custom-call(s32[344,128]{1,0:T(8,128)} %copy-done, s32[192]{0:T(256)} %copy-done.1, s32[192]{0:T(256)} %copy-done.2, s32[344,128]{1,0:T(8,128)} %copy-done, s32[48,128]{1,0:T(8,128)} %bitcast.7, bf16[6144,128]{1,0:T(8,128)(2,1)} %embed_hbm.1, f32[6144,128]{1,0:T(8,128)} %cotangent_hbm.1, ...), custom_call_target="tpu_custom_call" | custom-call | tf_op jit(solution)/shard_map/hops/pallas_call | solution.py:430
  79.1 1.1 %copy.16 = bf16[6144,128]{1,0:T(8,128)(2,1)} copy(bf16[6144,128]{1,0:T(8,128)(2,1)S(1)} %get-tuple-element.2) | data formatting | bytes 3145728
  80.3 1.7 %copy.17 = f32[6144,128]{1,0:T(8,128)} copy(f32[6144,128]{1,0:T(8,128)S(1)} %get-tuple-element.3) | data formatting | bytes 6291456
  (4 shorter events, 0.0 us)
Async XLA Ops:
  1.5 4.2 %copy-start.1 = (s32[192]{0:T(256)}, s32[192]{0:T(256)S(1)}, u32[]{:S(2)}) copy-start(s32[192]{0:T(256)S(1)} %reshape.26.inner_src) | copy-start | bytes 2308
  2.4 3.3 %copy-start.2 = (s32[192]{0:T(256)}, s32[192]{0:T(256)S(1)}, u32[]{:S(2)}) copy-start(s32[192]{0:T(256)S(1)} %reshape.27.border_src) | copy-start | bytes 2308
  5.7 0.7 copy-start
